TPU v7x, 32 devices: a whole 2x2x4 slice. The times are simulated.
32 devices in a mesh: wide: 8 (over z, y), narrow: 4 (over x, core).
Axes of the slice: x: 2, y: 2, z: 4, core: 2. Of those that a mesh axis runs over, the one named last changes fastest.
Arguments:
- patches: bfloat16 [2048, 1280], P('wide', 'narrow'), may hold values from -6 to 6
- window_ids: int32 [8, 64], P('wide'), may hold values from 0 to 31, never falling along the last dimension, each value on 1 to 16 neighbouring positions
- vit_gain: float32 [1280], replicated, may hold values from 0.25 to 1.75
- vit_qkv: bfloat16 [3, 1280, 1280], P(None, None, 'narrow'), may hold values from -0.15625 to 0.15625
- vit_qkv_bias: float32 [3, 1280], P(None, 'narrow'), may hold values from -3 to 3
- vit_proj: bfloat16 [1280, 1280], P('narrow'), may hold values from -0.15625 to 0.15625
- vit_proj_bias: float32 [1280], replicated, may hold values from -3 to 3
- merge_gain: float32 [1280], replicated, may hold values from 0.25 to 1.75
- merge_up: bfloat16 [5120, 5120], P(None, 'narrow'), may hold values from -0.078125 to 0.078125
- merge_up_bias: float32 [5120], P('narrow'), may hold values from -3 to 3
- merge_down: bfloat16 [5120, 8192], P('narrow'), may hold values from -0.078125 to 0.078125
- merge_down_bias: float32 [8192], replicated, may hold values from -3 to 3
- input_gain: float32 [8192], replicated, may hold values from 0.25 to 1.75
- kv_weight: bfloat16 [2, 8192, 1024], P(None, None, 'narrow'), may hold values from -0.0625 to 0.0625
- kv_bias: float32 [2, 1024], P(None, 'narrow'), may hold values from -3 to 3
- key_positions: int32 [3, 512], P(None, 'wide'), may hold values from 0 to 8191
- queries: bfloat16 [32, 64, 8192], P('wide', None, 'narrow'), may hold values from -70 to 70
- question_kv: bfloat16 [2, 32, 64, 1024], P(None, 'wide', None, 'narrow'), may hold values from -8 to 8
- question_start: int32 [32], P('wide'), may hold values from 8192 to 16383
- question_length: int32 [32], P('wide'), may hold values from 1 to 64, 1280 in all
Outputs:
- attended: bfloat16 [32, 64, 8192], P('wide', None, 'narrow')
- kv_cache: bfloat16 [2, 512, 1024], P(None, 'wide', 'narrow')
Inputs may be any that keep to these rules, and one draw needn't show every extreme that they name: `window_ids`: each row holds the window numbers of one index of wide's merged tokens in order; numbers never fall along a row, a window holds 1 to 16 merged tokens, and some window holds exactly 16. `question_length`: some question has all 64 tokens live.
All inputs are finite; a program needn't handle non-finite values. No bound on the sum of `question_length` on one device may be relied on, other than what follows from the above.
Results may differ from a plain program's by a relative error of at most 0.024.
Values may be sent and summed in bfloat16 or wider, within the bound.
A program may use at most 320 MiB of HBM per device.

v0:
```python
import jax
import jax.numpy as jnp
from jax import lax
from jax.sharding import PartitionSpec as P

HD = 128
VHD = 80
QLEN = 64
WIN_MERGED = 16


def rms_scale(values_in, gain):
    return (
        values_in
        * lax.rsqrt(jnp.mean(values_in * values_in, axis=-1, keepdims=True) + 1e-06)
        * gain
    )


def rotate_pairs(values_in, cosine, sine_part):
    half_dim = values_in.shape[-1] // 2
    first = values_in[..., :half_dim]
    second = values_in[..., half_dim:]
    return jnp.concatenate(
        [first * cosine - second * sine_part, second * cosine + first * sine_part], axis=-1
    )


def inverse_freq(head_dim):
    return jnp.power(
        jnp.float32(1000000.0), -jnp.arange(head_dim // 2, dtype=jnp.float32) * 2.0 / head_dim
    )


def mrope_angles(positions, head_dim):
    freqs = inverse_freq(head_dim)
    first_cut = head_dim // 8
    second_cut = first_cut + 3 * head_dim // 16
    place = positions.astype(jnp.float32)
    return jnp.concatenate(
        [
            place[0][:, None] * freqs[:first_cut],
            place[1][:, None] * freqs[first_cut:second_cut],
            place[2][:, None] * freqs[second_cut:],
        ],
        axis=-1,
    )


def window_attention(query_rows, key_rows, value_rows, patch_ids):
    row_count = query_rows.shape[0]
    heads_here = query_rows.shape[1] // VHD
    block_rows = min(256, row_count)
    margin = 4 * WIN_MERGED
    span = block_rows + 2 * margin
    key_pad = jnp.pad(key_rows, ((margin, margin), (0, 0)))
    value_pad = jnp.pad(value_rows, ((margin, margin), (0, 0)))
    ids_pad = jnp.pad(patch_ids, (margin, margin), constant_values=-1)
    query_block = query_rows.reshape(block_rows, heads_here, VHD)
    key_block = key_pad.reshape(span, heads_here, VHD)
    value_block = value_pad.reshape(span, heads_here, VHD)
    scores = jnp.einsum(
        "phd,shd->hps", query_block, key_block, preferred_element_type=jnp.float32
    ) * VHD ** (-0.5)
    keep_mask = patch_ids[:, None] == ids_pad[None, :]
    weights_f = jnp.where(keep_mask[None], jnp.exp(scores), jnp.float32(0.0))
    denom = jnp.sum(weights_f, axis=-1)
    mixed = (
        jnp.einsum(
            "hps,shd->phd",
            weights_f.astype(jnp.bfloat16),
            value_block,
            preferred_element_type=jnp.float32,
        )
        / jnp.transpose(denom)[:, :, None]
    )
    outputs = mixed.reshape(block_rows, heads_here * VHD).astype(jnp.bfloat16)
    return outputs


def per_device(
    patches,
    window_ids,
    vit_gain,
    vit_qkv,
    vit_qkv_bias,
    vit_proj,
    vit_proj_bias,
    merge_gain,
    merge_up,
    merge_up_bias,
    merge_down,
    merge_down_bias,
    input_gain,
    kv_weight,
    kv_bias,
    key_positions,
    queries,
    question_kv,
    question_start,
    question_length,
):
    vision_width = vit_gain.shape[0]
    whole_rows = lax.all_gather(patches, "narrow", axis=1, tiled=True)
    resid = whole_rows.astype(jnp.float32)
    normed = rms_scale(resid, vit_gain).astype(jnp.bfloat16)
    projected = [
        (
            jnp.dot(normed, vit_qkv[which], preferred_element_type=jnp.float32)
            + vit_qkv_bias[which]
        ).astype(jnp.bfloat16)
        for which in range(3)
    ]
    ids_patch = jnp.repeat(window_ids[0], 4)
    heads_out = window_attention(projected[0], projected[1], projected[2], ids_patch)
    vit_partial = jnp.dot(heads_out, vit_proj, preferred_element_type=jnp.float32)
    vit_total = lax.psum(vit_partial, "narrow")
    hidden = resid + (vit_total + vit_proj_bias)
    merged_rows = rms_scale(hidden, merge_gain).astype(jnp.bfloat16)
    merged_in = merged_rows.reshape(-1, 4 * vision_width)
    up_act = jax.nn.gelu(
        jnp.dot(merged_in, merge_up, preferred_element_type=jnp.float32) + merge_up_bias,
        approximate=False,
    ).astype(jnp.bfloat16)
    embed_partial = jnp.dot(up_act, merge_down, preferred_element_type=jnp.float32)
    embed_total = lax.psum(embed_partial, "narrow")
    embed_normed = rms_scale(embed_total + merge_down_bias, input_gain).astype(jnp.bfloat16)
    key_raw = jnp.dot(embed_normed, kv_weight[0], preferred_element_type=jnp.float32) + kv_bias[0]
    value_rows = (
        jnp.dot(embed_normed, kv_weight[1], preferred_element_type=jnp.float32) + kv_bias[1]
    ).astype(jnp.bfloat16)
    kv_heads_dev = key_raw.shape[1] // HD
    angles = mrope_angles(key_positions, HD)[:, None, :]
    key_rows = (
        rotate_pairs(key_raw.reshape(-1, kv_heads_dev, HD), jnp.cos(angles), jnp.sin(angles))
        .astype(jnp.bfloat16)
        .reshape(-1, kv_heads_dev * HD)
    )
    kv_cache = jnp.stack([key_rows, value_rows])
    q_count = queries.shape[0]
    heads_dev = queries.shape[2] // HD
    group_size = heads_dev // kv_heads_dev
    score_scale = HD ** (-0.5)
    token_place = (question_start[:, None] + jnp.arange(QLEN, dtype=jnp.int32)[None, :]).astype(
        jnp.float32
    )
    query_angle = token_place[:, :, None, None] * inverse_freq(HD)
    query_cos = jnp.cos(query_angle)
    query_sin = jnp.sin(query_angle)
    query_rot = rotate_pairs(
        queries.astype(jnp.float32).reshape(q_count, QLEN, heads_dev, HD), query_cos, query_sin
    ).astype(jnp.bfloat16)
    own_keys = rotate_pairs(
        question_kv[0].astype(jnp.float32).reshape(q_count, QLEN, kv_heads_dev, HD),
        query_cos,
        query_sin,
    ).astype(jnp.bfloat16)
    own_values = question_kv[1].reshape(q_count, QLEN, kv_heads_dev, HD)
    query_group = query_rot.reshape(q_count, QLEN, kv_heads_dev, group_size, HD)
    causal = jnp.arange(QLEN)[:, None] >= jnp.arange(QLEN)[None, :]
    own_scores = (
        jnp.einsum("qtkgd,qjkd->qkgtj", query_group, own_keys, preferred_element_type=jnp.float32)
        * score_scale
    )
    own_scores = jnp.where(causal, own_scores, -1e30)
    own_top = jnp.max(own_scores, axis=-1)
    own_w = jnp.exp(own_scores - own_top[..., None])
    own_sum = jnp.sum(own_w, axis=-1)
    own_acc = jnp.einsum(
        "qkgtj,qjkd->qkgtd",
        own_w.astype(jnp.bfloat16),
        own_values,
        preferred_element_type=jnp.float32,
    )
    piece_keys = lax.all_gather(key_rows, "wide", axis=0, tiled=True).reshape(-1, kv_heads_dev, HD)
    piece_values = lax.all_gather(value_rows, "wide", axis=0, tiled=True).reshape(
        -1, kv_heads_dev, HD
    )
    scores = (
        jnp.einsum("qtkgd,nkd->qkgtn", query_group, piece_keys, preferred_element_type=jnp.float32)
        * score_scale
    )
    new_top = jnp.maximum(own_top, jnp.max(scores, axis=-1))
    weights_f = jnp.exp(scores - new_top[..., None])
    shrink = jnp.exp(own_top - new_top)
    new_acc = own_acc * shrink[..., None] + jnp.einsum(
        "qkgtn,nkd->qkgtd",
        weights_f.astype(jnp.bfloat16),
        piece_values,
        preferred_element_type=jnp.float32,
    )
    denom = own_sum * shrink + jnp.sum(weights_f, axis=-1)
    mixed = new_acc / denom[..., None]
    mixed = jnp.transpose(mixed, (0, 3, 1, 2, 4)).reshape(q_count, QLEN, heads_dev * HD)
    live = jnp.arange(QLEN, dtype=jnp.int32)[None, :] < question_length[:, None]
    attended = jnp.where(live[:, :, None], mixed, jnp.float32(0.0)).astype(jnp.bfloat16)
    return (attended, kv_cache)


def solution(mesh):
    return jax.shard_map(
        per_device,
        mesh=mesh,
        in_specs=(
            P("wide", "narrow"),
            P("wide", None),
            P(),
            P(None, None, "narrow"),
            P(None, "narrow"),
            P("narrow", None),
            P(),
            P(),
            P(None, "narrow"),
            P("narrow"),
            P("narrow", None),
            P(),
            P(),
            P(None, None, "narrow"),
            P(None, "narrow"),
            P(None, "wide"),
            P("wide", None, "narrow"),
            P(None, "wide", None, "narrow"),
            P("wide"),
            P("wide"),
        ),
        out_specs=(P("wide", None, "narrow"), P(None, "wide", "narrow")),
        check_vma=False,
    )
```

profile of v0, /device:TPU:0, one launch (start us, length us, event | category | flops | bytes accessed | tf_op | source)
XLA Modules:
  0.0 229.1 jit_solution(9944364983503288775)
XLA Ops:
  7.2 0.8 slice_reduce_fusion
  8.1 0.7 broadcast_in_dim.31
  9.1 9.5 %all_gather.9 = bf16[256,1280]{0,1:T(8,128)(2,1)S(1)} all-gather(bf16[256,320]{0,1:T(8,128)(2,1)} %param.20), channel_id=1, replica_groups=mesh['wide'=8,'narrow'=4] {'narrow'}, dimensions={1}, use_global_device_ids=true | all-gather | bytes 819200 | tf_op jit(solution)/shard_map/all_gather | solution.py:104
  18.7 0.2 copy.66
  18.9 0.2 fusion.14
  19.1 1.8 fusion.20
  20.9 0.5 fusion.21
  21.4 0.5 fusion.19
  21.9 0.1 pad.13
  22.1 0.1 pad.11
  22.2 0.7 fusion.69
  22.9 0.4 fusion.18
  23.3 1.6 fusion.71
  25.0 0.2 all-reduce.8.cloned.1.call-start
  25.4 0.5 multiply_cosine_fusion
  26.1 0.3 fusion.66
  26.5 0.3 copy.92
  26.7 0.7 fusion.64
  27.7 2.4 %subtract_convert_fusion = (bf16[4,64,16,64]{3,1,2,0:T(8,128)(2,1)S(1)}, bf16[4,64,16,64]{3,1,2,0:T(8,128)(2,1)}) fusion(f32[4,64,16,64]{3,2,1,0:T(8,128)S(1)} %get-tuple-element.12, f32[4,64,16,64]{3,2,1,0:T(8,128)S(1)} %get-tuple-element.11, f32[4,64,64]{2,1,0:T(8,128)S(1)} %get-tuple-element.24, f32[4,64,64]{2,1,0:T(8,128)S(1)} %get-tuple-element.23), kind=kLoop, calls=%fused_computation.23 | loop fusion | flops 2097152 | bytes 3276800 | tf_op jit(solution)/shard_map/convert.5
  30.1 34.8 %all-reduce.6.cloned.1.call-done = f32[256,1280]{1,0:T(8,128)} async-done(((f32[256,1280]{1,0:T(8,128)}), f32[256,1280]{1,0:T(8,128)}) %all-reduce.6.cloned.1.call-update) | async-done | bytes 1310736 | tf_op jit(solution)/shard_map/psum | solution.py:117
  65.0 1.7 multiply_reduce_fusion.1
  66.7 0.3 multiply_convert_fusion.1
  67.0 0.4 reshape.298
  67.4 7.6 %fusion.44 = bf16[64,1280]{1,0:T(8,128)(2,1)S(1)} fusion(bf16[64,5120]{1,0:T(8,128)(2,1)S(1)} %reshape.298, bf16[5120,1280]{1,0:T(8,128)(2,1)} %param.28, f32[1280]{0:T(1024)S(1)} %copy-done.18), kind=kOutput, calls=%fused_computation.61 | convolution fusion | flops 844267520 | bytes 13931520 | tf_op jit(solution)/shard_map/dot_general | solution.py:122
  75.1 12.0 %fusion.72 = f32[64,8192]{1,0:T(8,128)} fusion(bf16[64,1280]{1,0:T(8,128)(2,1)S(1)} %fusion.44, bf16[1280,8192]{1,0:T(8,128)(2,1)} %param.30), kind=kOutput, calls=%fused_computation.126 | convolution fusion | flops 1342177280 | bytes 23232512 | tf_op jit(solution)/shard_map/dot_general | solution.py:125
  87.2 0.2 fusion.59
  87.4 0.9 copy-done.2
  88.3 1.3 fusion.70
  89.6 1.3 copy-done.3
  90.9 0.5 fusion.12
  91.5 47.1 %all-reduce.8.cloned.1.call-done = f32[64,8192]{1,0:T(8,128)} async-done(((f32[64,8192]{1,0:T(8,128)}), f32[64,8192]{1,0:T(8,128)}) %all-reduce.8.cloned.1.call-update) | async-done | bytes 2097168 | tf_op jit(solution)/shard_map/psum | solution.py:126
  138.7 2.0 multiply_reduce_fusion
  140.8 0.1 copy-done.6
  140.9 3.3 %fusion.22 = f32[64,256]{1,0:T(8,128)S(1)} fusion(bf16[2,8192,256]{2,1,0:T(8,128)(2,1)} %param.33, f32[256]{0:T(256)S(1)} %bitcast.134, f32[64,8192]{1,0:T(8,128)S(1)} %copy-done.6, f32[8192]{0:T(1024)S(1)} %copy-done.16, f32[64]{0:T(128)S(1)} %add_rsqrt_fusion.2, f32[8192]{0:T(1024)S(1)} %copy-done.9), kind=kOutput, calls=%fused_computation.44 | convolution fusion | flops 270548992 | bytes 6423808 | tf_op jit(solution)/shard_map/dot_general | solution.py:128
  144.3 0.2 multiply_subtract_fusion
  144.6 30.8 %all_gather.10 = bf16[512,256]{1,0:T(8,128)(2,1)S(1)} all-gather(bf16[64,256]{1,0:T(8,128)(2,1)S(1)} %bitcast.129), channel_id=1, replica_groups=mesh['wide'=8,'narrow'=4] {'wide'}, dimensions={0}, use_global_device_ids=true | all-gather | bytes 294912 | tf_op jit(solution)/shard_map/all_gather | solution.py:175
  175.4 0.1 copy.67
  175.6 3.7 %fusion.28 = bf16[64,256]{1,0:T(8,128)(2,1)S(1)} fusion(bf16[2,8192,256]{2,1,0:T(8,128)(2,1)} %param.33, f32[256]{0:T(256)S(1)} %bitcast.133, f32[64,8192]{1,0:T(8,128)} %all-reduce.8.cloned.1.call-done, f32[8192]{0:T(1024)S(1)} %copy-done.16, f32[64]{0:T(128)S(1)} %add_rsqrt_fusion.2, f32[8192]{0:T(1024)S(1)} %copy-done.9), kind=kOutput, calls=%fused_computation.46 | convolution fusion | flops 270565376 | bytes 6391040 | tf_op jit(solution)/shard_map/dot_general | solution.py:130
  179.3 30.7 %all_gather.11 = bf16[512,256]{1,0:T(8,128)(2,1)S(1)} all-gather(bf16[64,256]{1,0:T(8,128)(2,1)S(1)} %fusion.28), channel_id=1, replica_groups=mesh['wide'=8,'narrow'=4] {'wide'}, dimensions={0}, use_global_device_ids=true | all-gather | bytes 294912 | tf_op jit(solution)/shard_map/all_gather | solution.py:176
  210.1 1.5 bitcast_reduce_fusion
  211.6 2.2 fusion.1
  213.9 1.2 fusion.7
  215.1 0.3 copy-done.4
  215.5 1.8 fusion.11
  217.3 1.7 copy.76
  218.9 1.5 reshape.302
  220.4 0.6 pad_maximum_fusion.1
  221.1 1.2 select_convert_fusion
  (65 shorter events, 1.5 us)
Async XLA Ops:
  7.2 16.2 %copy-start = (bf16[320,1280]{1,0:T(8,128)(2,1)S(1)}, bf16[320,1280]{1,0:T(8,128)(2,1)}, u32[]{:S(2)}) copy-start(bf16[320,1280]{1,0:T(8,128)(2,1)} %param.25) | copy-start | bytes 2457604
  7.2 12.0 %copy-start.17 = (f32[1280]{0:T(1024)S(1)}, f32[1280]{0:T(1024)}, u32[]{:S(2)}) copy-start(f32[1280]{0:T(1024)} %param.22) | copy-start | bytes 15364
  7.2 57.8 %all-reduce.6.cloned.1.call-start = ((), (), s32[]{:S(2)}) async-start(), calls=%async_computation | async-start | bytes 2621440 | tf_op jit(solution)/shard_map/psum | solution.py:117
  18.9 2.0 copy-start.15
  23.3 2.0 copy-start.12
  23.3 2.0 copy-start.14
  23.3 2.6 %copy-start.8 = (bf16[2,4,64,256]{3,2,1,0:T(8,128)(2,1)S(1)}, bf16[2,4,64,256]{3,2,1,0:T(8,128)(2,1)}, u32[]{:S(2)}) copy-start(bf16[2,4,64,256]{3,2,1,0:T(8,128)(2,1)} %param.37) | copy-start | bytes 786436
  24.9 1.5 copy-start.7
  25.0 113.7 %all-reduce.8.cloned.1.call-start = ((), (), s32[]{:S(2)}) async-start(), calls=%async_computation.1 | async-start | bytes 4194304 | tf_op jit(solution)/shard_map/psum | solution.py:126
  27.7 37.3 %copy-start.10 = (f32[1280]{0:T(1024)S(1)}, f32[1280]{0:T(1024)}, u32[]{:S(2)}) copy-start(f32[1280]{0:T(1024)} %param.26) | copy-start | bytes 15364
  27.7 39.0 %copy-start.11 = (f32[1280]{0:T(1024)S(1)}, f32[1280]{0:T(1024)}, u32[]{:S(2)}) copy-start(f32[1280]{0:T(1024)} %param.27) | copy-start | bytes 15364
  65.0 1.7 copy-start.5
  66.7 0.7 copy-start.18
  87.1 1.2 copy-start.2
  89.6 1.3 copy-start.3
  89.6 1.9 copy-start.19
  89.6 1.9 copy-start.13
  89.6 49.1 %copy-start.9 = (f32[8192]{0:T(1024)S(1)}, f32[8192]{0:T(1024)}, u32[]{:S(2)}) copy-start(f32[8192]{0:T(1024)} %param.31) | copy-start | bytes 98308
  90.9 49.8 %copy-start.16 = (f32[8192]{0:T(1024)S(1)}, f32[8192]{0:T(1024)}, u32[]{:S(2)}) copy-start(f32[8192]{0:T(1024)} %param.32) | copy-start | bytes 98308
  138.7 2.2 copy-start.6
  213.9 1.6 copy-start.4
  217.3 5.0 %copy-start.1 = (bf16[320,1280]{1,0:T(8,128)(2,1)S(1)}, bf16[320,1280]{1,0:T(8,128)(2,1)}, u32[]{:S(2)}) copy-start(bf16[320,1280]{1,0:T(8,128)(2,1)} %param.25) | copy-start | bytes 2457604
Sparse Core Ops, SparseCore 0:
  25.1 39.8 all-reduce.5
  87.2 51.4 all-reduce.7
where the time goes:
time: 230 us; the launch traced here: 229 us
  waiting for transfers between devices  82 us (36%)
  blocking collectives  71.1 us (31%)
  matrix products  37.9 us (16%)
  between operations  14.5 us (6%)
  other arithmetic  12.9 us (6%)
  local copies, waits for them, and re-layouts  10.5 us (5%)
    psum x1, waiting for transfers between devices, per_device(): embed_total = lax.psum(embed_partial, 'narrow')  47.1 us
    psum x1, waiting for transfers between devices, per_device(): vit_total = lax.psum(vit_partial, 'narrow')  34.8 us
    all_gather x1, blocking collectives, per_device(): lax.all_gather(key_rows, 'wide', axis=0, tiled=True)  30.8 us
    all_gather x1, blocking collectives, per_device(): lax.all_gather(value_rows, 'wide', axis=0, tiled=True)  30.7 us
    dot_general x1, matrix products, per_device(): jnp.dot(up_act, merge_down, preferred_element_type=jnp.float32)  12 us
    all_gather x1, blocking collectives, per_device(): whole_rows = lax.all_gather(patches, 'narrow', axis=1, tiled=True)  9.54 us
    dot_general x1, matrix products, per_device(): jnp.dot(merged_in, merge_up, preferred_element_type=jnp.float32)  7.64 us
  transfers between devices with their start and end apart: 2, of which 2 were waited for; matrix products, arithmetic and copies ran while one was open for 3% of the time, Pallas kernels for 0%

commit v1 on v0

v1 whole, which is shorter than its diff:
```python
import functools

import jax
import jax.numpy as jnp
from jax import lax
from jax.experimental import pallas as pl
from jax.experimental.pallas import tpu as pltpu
from jax.sharding import PartitionSpec as P

HD = 128
VHD = 80
CHUNKS = 8
F32 = jnp.float32
BF16 = jnp.bfloat16
VMEM_LIMIT = 60 * 1024 * 1024


def dot(a, b):
    return jnp.dot(a, b, preferred_element_type=F32)


def dot_t(a, b):
    return lax.dot_general(a, b, (((1,), (1,)), ((), ())), preferred_element_type=F32)


def iota(shape, axis):
    return lax.broadcasted_iota(jnp.int32, shape, axis)


def vision_kernel(
    ids, patches, gain, qkv_bias, proj_bias, merge_gain, up_bias, down_bias, input_gain,
    kv_bias, cosine, sine,
    qkv_hbm, proj_hbm, up_hbm, down_hbm, kvw_hbm,
    kv_out,
    qkv_w, proj_w, up_w, down_w, kv_w, w_sem,
    rows, normed, heads, partial, give, got, x_give, x_got, merged, up_acc, up_act,
    d_part, d_give, d_got, dx_give, dx_got, emb, squares, kv_acc,
    send_sem, recv_sem,
):
    me = lax.axis_index("narrow")
    x, core = me // 2, me % 2
    cp = x * 2 + (1 - core)
    xp = (1 - x) * 2 + core
    dg = (1 - x) * 2 + (1 - core)
    row_count = patches.shape[0]
    part_w = patches.shape[1]
    width = proj_hbm.shape[1]
    block = row_count // 4
    merged_block = block // 4
    wide_d = down_hbm.shape[1]
    chunk = wide_d // CHUNKS

    def local(index, src, dst):
        return pltpu.make_async_copy(src, dst, w_sem.at[index])

    def remote(index, src, dst, peer):
        return pltpu.make_async_remote_copy(
            src_ref=src, dst_ref=dst, send_sem=send_sem.at[index], recv_sem=recv_sem.at[index],
            device_id={"narrow": peer}, device_id_type=pl.DeviceIdType.MESH,
        )

    loads = [
        local(0, qkv_hbm, qkv_w), local(1, proj_hbm, proj_w), local(2, up_hbm, up_w),
        local(3, down_hbm, down_w), local(4, kvw_hbm, kv_w),
    ]
    loads[0].start()
    loads[1].start()

    barrier = pltpu.get_barrier_semaphore()
    for peer in (cp, xp):
        pl.semaphore_signal(
            barrier, inc=1, device_id={"narrow": peer}, device_id_type=pl.DeviceIdType.MESH
        )
    pl.semaphore_wait(barrier, 2)

    sent = []

    def send(index, src, dst, peer):
        copy = remote(index, src, dst, peer)
        copy.start()
        sent.append(copy)

    def arrived(index, dst, peer):
        remote(index, dst, dst, peer).wait_recv()

    def gather_start(index, src, slots):
        send(index + 1, src, slots.at[me], xp)
        send(index, src, slots.at[me], cp)

    def gather_forward(index, slots):
        arrived(index + 1, slots.at[xp], xp)
        send(index + 2, slots.at[xp], slots.at[xp], cp)

    def gather_finish(index, slots):
        arrived(index, slots.at[cp], cp)
        arrived(index + 2, slots.at[dg], cp)

    gather_start(0, patches, rows)
    loads[2].start()
    rows[me] = patches[...]
    ids_row = ids[...].astype(F32)
    token_of = (iota((row_count, row_count // 4), 0) // 4 == iota((row_count, row_count // 4), 1))
    token_of = token_of.astype(F32)
    patch_col = jnp.sum(token_of * ids_row, axis=1, keepdims=True)
    patch_row = dot_t(
        jnp.broadcast_to(ids_row, (8, row_count // 4)).astype(BF16), token_of.astype(BF16)
    )[:1]
    same = patch_col == patch_row
    gather_forward(0, rows)
    gather_finish(0, rows)
    loads[3].start()
    loads[4].start()

    total_sq = jnp.zeros((row_count, 1), F32)
    for i in range(4):
        part = rows[i].astype(F32)
        total_sq += jnp.sum(part * part, axis=1, keepdims=True)
    scale = lax.rsqrt(total_sq / width + 1e-06)
    for i in range(4):
        normed[i] = (rows[i].astype(F32) * scale * gain[i]).astype(BF16)
    loads[0].wait()
    qkv = []
    for which in range(3):
        acc = dot(normed[0], qkv_w[which, :part_w])
        for i in range(1, 4):
            acc += dot(normed[i], qkv_w[which, part_w * i : part_w * (i + 1)])
        qkv.append((acc + qkv_bias[which]).astype(BF16))
    query, key, value = qkv
    lane = iota((1, part_w), 1)
    out = jnp.zeros((row_count, part_w), F32)
    for h in range(part_w // VHD):
        mine = ((lane >= VHD * h) & (lane < VHD * (h + 1))).astype(F32)
        scores = dot_t(query * mine.astype(BF16), key) * VHD ** (-0.5)
        weights = jnp.where(same, jnp.exp(scores), 0.0)
        denom = 1.0 / jnp.sum(weights, axis=1, keepdims=True)
        out += dot(weights.astype(BF16), value) * denom * mine
    heads[...] = out.astype(BF16)
    loads[1].wait()
    partial[...] = dot(heads[...], proj_w[...])

    def rows_of(ref, index, size):
        return ref[pl.ds(pl.multiple_of(index * size, size), size), :]

    give[0] = rows_of(partial, dg, block).astype(BF16)
    send(3, give.at[0], got.at[0], cp)
    give[1] = rows_of(partial, cp, block).astype(BF16)
    send(4, give.at[1], got.at[1], cp)
    resid = jnp.zeros((block, width), F32)
    for i in range(4):
        place = (iota((part_w, width), 1) - part_w * i == iota((part_w, width), 0))
        mine_rows = rows[i, pl.ds(pl.multiple_of(me * block, block), block), :]
        resid += dot(mine_rows, place.astype(F32).astype(BF16))
    resid = resid + proj_bias[...]
    arrived(3, got.at[0], cp)
    x_give[...] = (rows_of(partial, xp, block) + got[0].astype(F32)).astype(BF16)
    send(5, x_give, x_got, xp)
    arrived(4, got.at[1], cp)
    hidden = resid + rows_of(partial, me, block) + got[1].astype(F32)
    arrived(5, x_got, xp)
    hidden = hidden + x_got[...].astype(F32)
    hidden_sq = jnp.sum(hidden * hidden, axis=1, keepdims=True) / width
    hidden_n = (hidden * lax.rsqrt(hidden_sq + 1e-06) * merge_gain[...]).astype(BF16)
    to_row = iota((block, block), 0)
    order = (to_row % merged_block) * 4 + to_row // merged_block == iota((block, block), 1)
    ordered = dot(order.astype(F32).astype(BF16), hidden_n).astype(BF16)
    for j in range(4):
        merged[me, :, width * j : width * (j + 1)] = ordered[
            merged_block * j : merged_block * (j + 1)
        ]
    gather_start(6, merged.at[me], merged)
    gather_forward(6, merged)
    gather_finish(6, merged)

    loads[2].wait()
    up_acc[...] = jnp.zeros_like(up_acc)
    step = 512

    @pl.loop(0, up_hbm.shape[0] // step)
    def _(kk):
        at = pl.ds(pl.multiple_of(kk * step, step), step)
        up_acc[...] += dot(merged[:, :, at].reshape(block, step), up_w[at, :])

    pre = up_acc[...] + up_bias[...]
    up_act[...] = (0.5 * pre * (1.0 + lax.erf(pre * 0.7071067811865476))).astype(BF16)
    loads[3].wait()
    kv_acc[...] = jnp.zeros_like(kv_acc)
    square_sum = jnp.zeros((merged_block, 1), F32)
    for t in range(CHUNKS + 4):
        c = t
        if c < CHUNKS:
            d_part[c] = dot(up_act[...], down_w[:, chunk * c : chunk * (c + 1)])
            d_give[c, 0] = rows_of(d_part.at[c], dg, merged_block).astype(BF16)
            d_give[c, 1] = rows_of(d_part.at[c], cp, merged_block).astype(BF16)
            send(12 + 5 * c, d_give.at[c], d_got.at[c], cp)
        c = t - 1
        if 0 <= c < CHUNKS:
            arrived(12 + 5 * c, d_got.at[c], cp)
            dx_give[c] = (
                rows_of(d_part.at[c], xp, merged_block) + d_got[c, 0].astype(F32)
            ).astype(BF16)
            send(13 + 5 * c, dx_give.at[c], dx_got.at[c], xp)
        c = t - 2
        if 0 <= c < CHUNKS:
            arrived(13 + 5 * c, dx_got.at[c], xp)
            cols = slice(chunk * c, chunk * (c + 1))
            embed = rows_of(d_part.at[c], me, merged_block) + d_got[c, 1].astype(F32)
            embed = embed + dx_got[c].astype(F32) + down_bias[:, cols]
            square_sum += jnp.sum(embed * embed, axis=1, keepdims=True)
            emb[c, me] = (embed * input_gain[:, cols]).astype(BF16)
            gather_start(14 + 5 * c, emb.at[c, me], emb.at[c])
            if c == CHUNKS - 1:
                squares[me] = jnp.broadcast_to(square_sum, squares.shape[1:])
                gather_start(9, squares.at[me], squares)
        c = t - 3
        if 0 <= c < CHUNKS:
            gather_forward(14 + 5 * c, emb.at[c])
            if c == CHUNKS - 1:
                gather_forward(9, squares)
        c = t - 4
        if 0 <= c < CHUNKS:
            gather_finish(14 + 5 * c, emb.at[c])
            if c == 0:
                loads[4].wait()
            lhs = emb[c].reshape(block, chunk)
            for which in range(2):
                kv_acc[which] += dot(lhs, kv_w[which, chunk * c : chunk * (c + 1), :])
    gather_finish(9, squares)
    row_scale = lax.rsqrt(squares[...].reshape(block, squares.shape[2]) / wide_d + 1e-06)
    for h in range(kv_w.shape[2] // HD):
        cols = slice(HD * h, HD * (h + 1))
        raw = kv_acc[0, :, cols] * row_scale + kv_bias[0, :, cols]
        rotated = raw * cosine[...] + pltpu.roll(raw, HD // 2, 1) * sine[...]
        kv_out[0, :, cols] = rotated.astype(BF16)
        kv_out[1, :, cols] = (kv_acc[1, :, cols] * row_scale + kv_bias[1, :, cols]).astype(BF16)
    for copy in sent:
        copy.wait_send()


def wide_gather_kernel(count, kv, out, local_sem, send_sem, recv_sem):
    me = lax.axis_index("wide")

    def peer_at(offset):
        return lax.rem(me + offset, count)

    def remote(offset):
        return pltpu.make_async_remote_copy(
            src_ref=kv, dst_ref=out.at[me],
            send_sem=send_sem.at[offset - 1], recv_sem=recv_sem.at[offset - 1],
            device_id={"wide": peer_at(offset)}, device_id_type=pl.DeviceIdType.MESH,
        )

    mine = pltpu.make_async_copy(kv, out.at[me], local_sem)
    mine.start()
    barrier = pltpu.get_barrier_semaphore()

    @pl.loop(1, count)
    def _(offset):
        pl.semaphore_signal(
            barrier, inc=1, device_id={"wide": peer_at(offset)},
            device_id_type=pl.DeviceIdType.MESH,
        )

    pl.semaphore_wait(barrier, count - 1)

    @pl.loop(1, count)
    def _(offset):
        remote(offset).start()

    mine.wait()

    @pl.loop(1, count)
    def _(offset):
        copy = remote(offset)
        copy.wait_send()
        copy.wait_recv()


def attention_kernel(
    length, queries, own_kv, cosine, sine, kv_all, out, rotated
):
    question = pl.program_id(0)
    tokens = queries.shape[1]
    groups = queries.shape[2] // HD
    keys_n = kv_all.shape[0] * kv_all.shape[2]
    cos, sin = cosine[0], sine[0]

    def rotate(rows):
        rows = rows.astype(F32)
        return (rows * cos + pltpu.roll(rows, HD // 2, 1) * sin).astype(BF16)

    own_key = rotate(own_kv[0, 0])
    for g in range(groups):
        rotated[tokens * g : tokens * (g + 1), :] = rotate(queries[0, :, HD * g : HD * (g + 1)])
    query = rotated[...]
    rows_n = tokens * groups
    factor = HD ** (-0.5)
    own = dot_t(query, own_key) * factor
    token = iota((rows_n, tokens), 0) % tokens
    own = jnp.where(token >= iota((rows_n, tokens), 1), own, -1e30)
    scores = dot_t(query, kv_all[:, 0].reshape(keys_n, HD)) * factor
    top = jnp.maximum(
        jnp.max(scores, axis=1, keepdims=True), jnp.max(own, axis=1, keepdims=True)
    )
    weights = jnp.exp(scores - top)
    own_w = jnp.exp(own - top)
    denom = jnp.sum(weights, axis=1, keepdims=True) + jnp.sum(own_w, axis=1, keepdims=True)
    mixed = dot(weights.astype(BF16), kv_all[:, 1].reshape(keys_n, HD))
    mixed += dot(own_w.astype(BF16), own_kv[1, 0])
    live = iota((rows_n, HD), 0) % tokens < length[question]
    mixed = jnp.where(live, mixed * (1.0 / denom), 0.0).astype(BF16)
    for g in range(groups):
        out[0, :, HD * g : HD * (g + 1)] = mixed[tokens * g : tokens * (g + 1)]


def inverse_freq(head_dim):
    return jnp.power(
        jnp.float32(1000000.0), -jnp.arange(head_dim // 2, dtype=F32) * 2.0 / head_dim
    )


def mrope_angles(positions, head_dim):
    freqs = inverse_freq(head_dim)
    first_cut = head_dim // 8
    second_cut = first_cut + 3 * head_dim // 16
    place = positions.astype(F32)
    return jnp.concatenate(
        [
            place[0][:, None] * freqs[:first_cut],
            place[1][:, None] * freqs[first_cut:second_cut],
            place[2][:, None] * freqs[second_cut:],
        ],
        axis=-1,
    )


def turns(angles):
    cosine, sine = jnp.cos(angles), jnp.sin(angles)
    return (
        jnp.concatenate([cosine, cosine], axis=-1),
        jnp.concatenate([-sine, sine], axis=-1),
    )


def per_device(
    n_wide,
    patches,
    window_ids,
    vit_gain,
    vit_qkv,
    vit_qkv_bias,
    vit_proj,
    vit_proj_bias,
    merge_gain,
    merge_up,
    merge_up_bias,
    merge_down,
    merge_down_bias,
    input_gain,
    kv_weight,
    kv_bias,
    key_positions,
    queries,
    question_kv,
    question_start,
    question_length,
):
    rows_n, part_w = patches.shape
    width = vit_proj.shape[1]
    block = rows_n // 4
    merged_block = block // 4
    d_wide = merge_down.shape[1]
    chunk = d_wide // CHUNKS
    hidden_n = merge_up.shape[1]
    kv_w = kv_weight.shape[2]
    key_cos, key_sin = turns(mrope_angles(key_positions, HD))
    tokens = queries.shape[1]
    place = (question_start[:, None] + jnp.arange(tokens, dtype=jnp.int32)[None, :]).astype(F32)
    query_cos, query_sin = turns(place[:, :, None] * inverse_freq(HD))

    vmem = pl.BlockSpec(memory_space=pltpu.VMEM)
    hbm = pl.BlockSpec(memory_space=pl.ANY)
    copies = 12 + 5 * CHUNKS
    kv_cache = pl.pallas_call(
        vision_kernel,
        out_shape=jax.ShapeDtypeStruct((2, block, kv_w), BF16),
        in_specs=[vmem] * 12 + [hbm] * 5,
        out_specs=vmem,
        scratch_shapes=[
            pltpu.VMEM(vit_qkv.shape, BF16),
            pltpu.VMEM(vit_proj.shape, BF16),
            pltpu.VMEM(merge_up.shape, BF16),
            pltpu.VMEM(merge_down.shape, BF16),
            pltpu.VMEM(kv_weight.shape, BF16),
            pltpu.SemaphoreType.DMA((5,)),
            pltpu.VMEM((4, rows_n, part_w), BF16),
            pltpu.VMEM((4, rows_n, part_w), BF16),
            pltpu.VMEM((rows_n, part_w), BF16),
            pltpu.VMEM((rows_n, width), F32),
            pltpu.VMEM((2, block, width), BF16),
            pltpu.VMEM((2, block, width), BF16),
            pltpu.VMEM((block, width), BF16),
            pltpu.VMEM((block, width), BF16),
            pltpu.VMEM((4, merged_block, 4 * width), BF16),
            pltpu.VMEM((block, hidden_n), F32),
            pltpu.VMEM((block, hidden_n), BF16),
            pltpu.VMEM((CHUNKS, block, chunk), F32),
            pltpu.VMEM((CHUNKS, 2, merged_block, chunk), BF16),
            pltpu.VMEM((CHUNKS, 2, merged_block, chunk), BF16),
            pltpu.VMEM((CHUNKS, merged_block, chunk), BF16),
            pltpu.VMEM((CHUNKS, merged_block, chunk), BF16),
            pltpu.VMEM((CHUNKS, 4, merged_block, chunk), BF16),
            pltpu.VMEM((4, merged_block, HD), F32),
            pltpu.VMEM((2, block, kv_w), F32),
            pltpu.SemaphoreType.DMA((copies,)),
            pltpu.SemaphoreType.DMA((copies,)),
        ],
        compiler_params=pltpu.CompilerParams(
            collective_id=0, has_side_effects=True, vmem_limit_bytes=VMEM_LIMIT
        ),
        name="vision_to_kv",
    )(
        window_ids,
        patches,
        vit_gain.reshape(4, 1, part_w),
        vit_qkv_bias.reshape(3, 1, part_w),
        vit_proj_bias.reshape(1, width),
        merge_gain.reshape(1, width),
        merge_up_bias.reshape(1, hidden_n),
        merge_down_bias.reshape(1, d_wide),
        input_gain.reshape(1, d_wide),
        kv_bias.reshape(2, 1, kv_w),
        key_cos,
        key_sin,
        vit_qkv,
        vit_proj,
        merge_up,
        merge_down,
        kv_weight,
    )
    kv_all = pl.pallas_call(
        functools.partial(wide_gather_kernel, n_wide),
        out_shape=jax.ShapeDtypeStruct((n_wide, 2, block, kv_w), BF16),
        in_specs=[hbm],
        out_specs=hbm,
        scratch_shapes=[
            pltpu.SemaphoreType.DMA,
            pltpu.SemaphoreType.DMA((n_wide - 1,)),
            pltpu.SemaphoreType.DMA((n_wide - 1,)),
        ],
        compiler_params=pltpu.CompilerParams(collective_id=1, has_side_effects=True),
        name="kv_over_wide",
    )(kv_cache)
    q_count = queries.shape[0]
    kv_heads = kv_w // HD
    group_w = queries.shape[2] // kv_heads
    attended = pl.pallas_call(
        attention_kernel,
        grid_spec=pltpu.PrefetchScalarGridSpec(
            num_scalar_prefetch=1,
            grid=(q_count, kv_heads),
            in_specs=[
                pl.BlockSpec((1, tokens, group_w), lambda q, h, n: (q, 0, h)),
                pl.BlockSpec((2, 1, tokens, HD), lambda q, h, n: (0, q, 0, h)),
                pl.BlockSpec((1, tokens, HD), lambda q, h, n: (q, 0, 0)),
                pl.BlockSpec((1, tokens, HD), lambda q, h, n: (q, 0, 0)),
                pl.BlockSpec((n_wide, 2, block, HD), lambda q, h, n: (0, 0, 0, h)),
            ],
            out_specs=pl.BlockSpec((1, tokens, group_w), lambda q, h, n: (q, 0, h)),
            scratch_shapes=[pltpu.VMEM((tokens * group_w // HD, HD), BF16)],
        ),
        out_shape=jax.ShapeDtypeStruct(queries.shape, BF16),
        compiler_params=pltpu.CompilerParams(vmem_limit_bytes=VMEM_LIMIT),
        name="question_attention",
    )(question_length, queries, question_kv, query_cos, query_sin, kv_all)
    return (attended, kv_cache)


def solution(mesh):
    return jax.shard_map(
        functools.partial(per_device, mesh.shape["wide"]),
        mesh=mesh,
        in_specs=(
            P("wide", "narrow"),
            P("wide", None),
            P(),
            P(None, None, "narrow"),
            P(None, "narrow"),
            P("narrow", None),
            P(),
            P(),
            P(None, "narrow"),
            P("narrow"),
            P("narrow", None),
            P(),
            P(),
            P(None, None, "narrow"),
            P(None, "narrow"),
            P(None, "wide"),
            P("wide", None, "narrow"),
            P(None, "wide", None, "narrow"),
            P("wide"),
            P("wide"),
        ),
        out_specs=(P("wide", None, "narrow"), P(None, "wide", "narrow")),
        check_vma=False,
    )
```

time: 230 us -> 102 us (0.44)
  the two profiles are of different devices: /device:TPU:0 before, /device:TPU:13 now
where the time goes in v1:
time: 102 us
  Pallas kernels  80.8 us (79%)
  local copies, waits for them, and re-layouts  16.3 us (16%)
  other arithmetic  3.9 us (4%)
    pallas_call x1, Pallas kernels, per_device(): pl.pallas_call(vision_kernel, out_shape=jax.ShapeDtypeStruct((2, block, k...  54.1 us
    pallas_call x1, Pallas kernels, per_device(): pl.pallas_call(functools.partial(wide_gather_kernel, n_wide), out_shape=j...  16.6 us
    pallas_call x1, Pallas kernels, per_device(): pl.pallas_call(attention_kernel, grid_spec=pltpu.PrefetchScalarGridSpec(n...  10.2 us
    unnamed x5, local copies, waits for them, and re-layouts  8.48 us

profile of v1, /device:TPU:13, one launch (start us, length us, event | category | flops | bytes accessed | tf_op | source)
XLA Modules:
  0.0 101.7 jit_solution(14255716481556342622)
XLA Ops:
  0.6 0.1 fusion.5
  0.7 0.7 convert_element_type.11
  1.4 0.1 broadcast_multiply_fusion
  1.5 0.1 broadcast_multiply_fusion.2
  1.6 0.2 fusion.3
  1.8 0.7 pad_maximum_fusion.4.sine
  2.5 0.7 pad_maximum_fusion.3.cosine
  3.2 5.3 %copy.23.qkv_hbm = bf16[3,1280,320]{2,1,0:T(8,128)(2,1)} copy(bf16[3,1280,320]{1,2,0:T(8,128)(2,1)} %param.23) | data formatting | bytes 4915200 | tf_op args[3]
  8.5 1.7 %copy.22.patches = bf16[256,320]{1,0:T(8,128)(2,1)} copy(bf16[256,320]{0,1:T(8,128)(2,1)} %param.20) | data formatting | bytes 327680 | tf_op args[0]
  10.2 1.4 %reshape.62.gain = f32[4,1,320]{2,1,0:T(1,128)} reshape(f32[1280]{0:T(1024)} %param.22) | data formatting | bytes 10240 | tf_op jit(solution)/shard_map/reshape | solution.py:424
  11.5 1.3 %reshape.64.proj_bias = f32[1,1280]{1,0:T(1,128)} reshape(f32[1280]{0:T(1024)} %param.26) | data formatting | bytes 10240 | tf_op jit(solution)/shard_map/reshape | solution.py:426
  12.8 1.3 %reshape.65.merge_gain = f32[1,1280]{1,0:T(1,128)} reshape(f32[1280]{0:T(1024)} %param.27) | data formatting | bytes 10240 | tf_op jit(solution)/shard_map/reshape | solution.py:427
  14.1 1.3 %reshape.66.up_bias = f32[1,1280]{1,0:T(1,128)} reshape(f32[1280]{0:T(1024)} %param.29) | data formatting | bytes 10240 | tf_op jit(solution)/shard_map/reshape | solution.py:428
  15.4 1.3 %reshape.63.qkv_bias = f32[3,1,320]{2,1,0:T(1,128)} reshape(f32[3,320]{1,0:T(4,128)} %param.24) | data formatting | bytes 7680 | tf_op jit(solution)/shard_map/reshape | solution.py:425
  16.7 1.3 %reshape.69.kv_bias = f32[2,1,256]{2,1,0:T(1,128)} reshape(f32[2,256]{1,0:T(2,128)} %param.34) | data formatting | bytes 4096 | tf_op jit(solution)/shard_map/reshape | solution.py:431
  18.0 0.0 copy-start
  18.0 54.1 %vision_to_kv.1.kv = bf16[2,64,256]{2,1,0:T(8,128)(2,1)} custom-call(s32[1,64]{1,0:T(1,128)} %ids.1, bf16[256,320]{1,0:T(8,128)(2,1)} %copy.22.patches, f32[4,1,320]{2,1,0:T(1,128)} %reshape.62.gain, f32[3,1,320]{2,1,0:T(1,128)} %reshape.63.qkv_bias, f32[1,1280]{1,0:T(1,128)} %reshape.64.proj_bias, f32[1,1280]{1,0:T(1,128)} %reshape.65.merge_gain, ...), custom_call_target="tpu_custom_call" | custom-call | tf_op jit(solution)/shard_map/vision_to_kv/pallas_call | solution.py:383
  72.0 16.6 %kv_over_wide.1.kv_all = bf16[8,2,64,256]{3,2,1,0:T(8,128)(2,1)} custom-call(bf16[2,64,256]{2,1,0:T(8,128)(2,1)} %vision_to_kv.1.kv), custom_call_target="tpu_custom_call" | custom-call | tf_op jit(solution)/shard_map/kv_over_wide/pallas_call | solution.py:440
  88.6 0.0 copy-done
  88.6 0.1 add_convert_fusion
  88.7 0.5 fusion
  89.2 0.8 pad_maximum_fusion
  90.1 10.2 %question_attention.1 = bf16[4,64,2048]{2,1,0:T(8,128)(2,1)} custom-call(s32[4]{0:T(128)} %length.1, bf16[4,64,2048]{2,1,0:T(8,128)(2,1)} %queries.1, bf16[2,4,64,256]{3,2,1,0:T(8,128)(2,1)} %own_kv.1, f32[4,64,128]{2,1,0:T(8,128)} %get-tuple-element.13.cosine, f32[4,64,128]{2,1,0:T(8,128)} %get-tuple-element.14.sine, bf16[8,2,64,256]{3,2,1,0:T(8,128)(2,1)} %kv_over_wide.1.kv_all), custom_call_target="tpu_custom_call" | custom-call | tf_op jit(solution)/shard_map/question_attention/pallas_call | solution.py:456
  100.2 1.5 %copy.25 = bf16[2,64,256]{2,1,0:T(8,128)(2,1)} copy(bf16[2,64,256]{2,1,0:T(8,128)(2,1)} %vision_to_kv.1.kv) | data formatting | bytes 131072
  (2 shorter events, 0.0 us)
Async XLA Ops:
  18.0 70.7 %copy-start = (s32[4]{0:T(128)S(1)}, s32[4]{0:T(128)}, u32[]{:S(2)}) copy-start(s32[4]{0:T(128)} %param.38) | copy-start | bytes 52

commit v2 on v1

v2 whole, which is shorter than its diff:
```python
import functools

import jax
import jax.numpy as jnp
import numpy as np
from jax import lax
from jax.experimental import pallas as pl
from jax.experimental.pallas import tpu as pltpu
from jax.sharding import PartitionSpec as P

HD = 128
VHD = 80
CHUNKS = 8
F32 = jnp.float32
BF16 = jnp.bfloat16
VMEM_LIMIT = 60 * 1024 * 1024


def dot(a, b):
    return jnp.dot(a, b, preferred_element_type=F32)


def dot_t(a, b):
    return lax.dot_general(a, b, (((1,), (1,)), ((), ())), preferred_element_type=F32)


def iota(shape, axis):
    return lax.broadcasted_iota(jnp.int32, shape, axis)


def dot_0(a, b):
    return lax.dot_general(a, b, (((0,), (0,)), ((), ())), preferred_element_type=F32)


def row(ref):
    return ref[...].reshape(1, ref.shape[0])


def column(values):
    n = values.shape[1]
    return jnp.sum(
        jnp.where(iota((n, n), 0) == iota((n, n), 1), values, 0.0), axis=1, keepdims=True
    )


def vision_kernel(
    n_wide,
    ids, patches, gain, qkv_bias, proj_bias, merge_gain, up_bias, down_bias, input_gain,
    kv_bias, cosine, sine,
    qkv_hbm, proj_hbm, up_hbm, down_hbm, kvw_hbm,
    kv_out, kv_all,
    qkv_w, proj_w, up_w, down_w, kv_w, w_sem,
    rows, normed, heads, partial, give, got, x_give, x_got, merged, up_acc, up_act,
    d_part, d_give, d_got, dx_give, dx_got, emb, squares, kv_acc,
    send_sem, recv_sem, o_send, o_recv, i_send, i_recv,
):
    me = lax.axis_index("narrow")
    x, core = me // 2, me % 2
    cp = x * 2 + (1 - core)
    xp = (1 - x) * 2 + core
    dg = (1 - x) * 2 + (1 - core)
    part_w, row_count = patches.shape
    width = proj_hbm.shape[1]
    block = row_count // 4
    merged_block = block // 4
    wide_d = down_hbm.shape[1]
    chunk = wide_d // CHUNKS
    wide = lax.axis_index("wide")
    outer_n = n_wide // 2
    outer, inner = wide // 2, wide % 2
    inner_peer = outer * 2 + (1 - inner)

    def outer_at(offset):
        return ((outer + offset) % outer_n) * 2 + inner

    def local(index, src, dst):
        return pltpu.make_async_copy(src, dst, w_sem.at[index])

    def remote(index, src, dst, peer):
        return pltpu.make_async_remote_copy(
            src_ref=src, dst_ref=dst, send_sem=send_sem.at[index], recv_sem=recv_sem.at[index],
            device_id={"narrow": peer}, device_id_type=pl.DeviceIdType.MESH,
        )

    loads = [
        local(0, qkv_hbm, qkv_w), local(1, proj_hbm, proj_w), local(2, up_hbm, up_w),
        local(3, down_hbm, down_w), local(4, kvw_hbm, kv_w),
    ]
    loads[0].start()
    loads[1].start()

    barrier = pltpu.get_barrier_semaphore()

    def greet(peer):
        pl.semaphore_signal(barrier, inc=1, device_id=peer, device_id_type=pl.DeviceIdType.MESH)

    greet({"narrow": cp})
    greet({"narrow": xp})
    greet({"wide": inner_peer})

    @pl.loop(1, outer_n)
    def _(offset):
        greet({"wide": outer_at(offset)})

    pl.semaphore_wait(barrier, outer_n + 2)

    sent = []

    def send(index, src, dst, peer):
        copy = remote(index, src, dst, peer)
        copy.start()
        sent.append(copy)

    def arrived(index, dst, peer):
        remote(index, dst, dst, peer).wait_recv()

    def gather_start(index, src, slots):
        send(index + 1, src, slots.at[me], xp)
        send(index, src, slots.at[me], cp)

    def gather_forward(index, slots):
        arrived(index + 1, slots.at[xp], xp)
        send(index + 2, slots.at[xp], slots.at[xp], cp)

    def gather_finish(index, slots):
        arrived(index, slots.at[cp], cp)
        arrived(index + 2, slots.at[dg], cp)

    gather_start(0, patches, rows)
    loads[2].start()
    rows[me] = patches[...]
    ids_row = ids[...].astype(F32)
    token_of = (iota((row_count, row_count // 4), 0) // 4 == iota((row_count, row_count // 4), 1))
    token_of = token_of.astype(F32)
    patch_col = jnp.sum(token_of * ids_row, axis=1, keepdims=True)
    patch_row = dot_t(
        jnp.broadcast_to(ids_row, (8, row_count // 4)).astype(BF16), token_of.astype(BF16)
    )[:1]
    same = patch_col == patch_row
    gather_forward(0, rows)
    gather_finish(0, rows)
    loads[3].start()
    loads[4].start()

    total_sq = jnp.zeros((1, row_count), F32)
    for i in range(4):
        part = rows[i].astype(F32)
        total_sq += jnp.sum(part * part, axis=0, keepdims=True)
    scale = lax.rsqrt(total_sq / width + 1e-06)
    features = rows[...].reshape(width, row_count)
    gains = row(gain)
    for i in range(0, width, 128):
        normed[i : i + 128, :] = (
            features[i : i + 128].astype(F32) * scale * column(gains[:, i : i + 128])
        ).astype(BF16)
    loads[0].wait()
    query, key, value = [
        (dot(qkv_w[which], normed[...]) + column(qkv_bias[which : which + 1, :])).astype(BF16)
        for which in range(3)
    ]
    for h in range(part_w // VHD):
        at = slice(VHD * h, VHD * (h + 1))
        scores = dot_0(key[at], query[at]) * VHD ** (-0.5)
        weights = jnp.where(same, jnp.exp(scores), 0.0)
        denom = 1.0 / jnp.sum(weights, axis=0, keepdims=True)
        heads[at, :] = (dot(value[at], weights.astype(BF16)) * denom).astype(BF16)
    loads[1].wait()
    partial[...] = dot_0(heads[...], proj_w[...])

    def rows_of(ref, index, size):
        return ref[pl.ds(pl.multiple_of(index * size, size), size), :]

    give[0] = rows_of(partial, dg, block).astype(BF16)
    send(3, give.at[0], got.at[0], cp)
    give[1] = rows_of(partial, cp, block).astype(BF16)
    send(4, give.at[1], got.at[1], cp)
    mine = iota((block, row_count), 1) - block * me == iota((block, row_count), 0)
    resid = dot_t(mine.astype(F32).astype(BF16), features) + row(proj_bias)
    arrived(3, got.at[0], cp)
    x_give[...] = (rows_of(partial, xp, block) + got[0].astype(F32)).astype(BF16)
    send(5, x_give, x_got, xp)
    arrived(4, got.at[1], cp)
    hidden = resid + rows_of(partial, me, block) + got[1].astype(F32)
    arrived(5, x_got, xp)
    hidden = hidden + x_got[...].astype(F32)
    hidden_sq = jnp.sum(hidden * hidden, axis=1, keepdims=True) / width
    hidden_n = (hidden * lax.rsqrt(hidden_sq + 1e-06) * row(merge_gain)).astype(BF16)
    to_row = iota((block, block), 0)
    order = (to_row % merged_block) * 4 + to_row // merged_block == iota((block, block), 1)
    ordered = dot(order.astype(F32).astype(BF16), hidden_n).astype(BF16)
    for j in range(4):
        merged[me, :, width * j : width * (j + 1)] = ordered[
            merged_block * j : merged_block * (j + 1)
        ]
    gather_start(6, merged.at[me], merged)
    gather_forward(6, merged)
    gather_finish(6, merged)

    loads[2].wait()
    up_acc[...] = jnp.zeros_like(up_acc)
    step = 512

    @pl.loop(0, up_hbm.shape[0] // step)
    def _(kk):
        at = pl.ds(pl.multiple_of(kk * step, step), step)
        up_acc[...] += dot(merged[:, :, at].reshape(block, step), up_w[at, :])

    pre = up_acc[...] + row(up_bias)
    up_act[...] = (0.5 * pre * (1.0 + lax.erf(pre * 0.7071067811865476))).astype(BF16)
    loads[3].wait()
    kv_acc[...] = jnp.zeros_like(kv_acc)
    square_sum = jnp.zeros((merged_block, 1), F32)
    for t in range(CHUNKS + 4):
        c = t
        if c < CHUNKS:
            d_part[c] = dot(up_act[...], down_w[:, chunk * c : chunk * (c + 1)])
            d_give[c, 0] = rows_of(d_part.at[c], dg, merged_block).astype(BF16)
            d_give[c, 1] = rows_of(d_part.at[c], cp, merged_block).astype(BF16)
            send(12 + 5 * c, d_give.at[c], d_got.at[c], cp)
        c = t - 1
        if 0 <= c < CHUNKS:
            arrived(12 + 5 * c, d_got.at[c], cp)
            dx_give[c] = (
                rows_of(d_part.at[c], xp, merged_block) + d_got[c, 0].astype(F32)
            ).astype(BF16)
            send(13 + 5 * c, dx_give.at[c], dx_got.at[c], xp)
        c = t - 2
        if 0 <= c < CHUNKS:
            arrived(13 + 5 * c, dx_got.at[c], xp)
            cols = slice(chunk * c, chunk * (c + 1))
            embed = rows_of(d_part.at[c], me, merged_block) + d_got[c, 1].astype(F32)
            embed = embed + dx_got[c].astype(F32) + down_bias[:, cols]
            square_sum += jnp.sum(embed * embed, axis=1, keepdims=True)
            emb[c, me] = (embed * input_gain[:, cols]).astype(BF16)
            gather_start(14 + 5 * c, emb.at[c, me], emb.at[c])
            if c == CHUNKS - 1:
                squares[me] = jnp.broadcast_to(square_sum, squares.shape[1:])
                gather_start(9, squares.at[me], squares)
        c = t - 3
        if 0 <= c < CHUNKS:
            gather_forward(14 + 5 * c, emb.at[c])
            if c == CHUNKS - 1:
                gather_forward(9, squares)
        c = t - 4
        if 0 <= c < CHUNKS:
            gather_finish(14 + 5 * c, emb.at[c])
            if c == 0:
                loads[4].wait()
            lhs = emb[c].reshape(block, chunk)
            for which in range(2):
                kv_acc[which] += dot(lhs, kv_w[which, chunk * c : chunk * (c + 1), :])
    gather_finish(9, squares)
    row_scale = lax.rsqrt(squares[...].reshape(block, squares.shape[2]) / wide_d + 1e-06)
    for h in range(kv_w.shape[2] // HD):
        cols = slice(HD * h, HD * (h + 1))
        raw = kv_acc[0, :, cols] * row_scale + kv_bias[0:1, cols]
        rotated = raw * cosine[...] + pltpu.roll(raw, HD // 2, 1) * sine[...]
        kv_out[0, :, cols] = rotated.astype(BF16)
        kv_out[1, :, cols] = (kv_acc[1, :, cols] * row_scale + kv_bias[1:2, cols]).astype(BF16)
    kv_all[wide] = kv_out[...]

    def along(offset, src, slot):
        return pltpu.make_async_remote_copy(
            src_ref=src, dst_ref=kv_all.at[slot],
            send_sem=o_send.at[offset - 1], recv_sem=o_recv.at[offset - 1],
            device_id={"wide": outer_at(offset)}, device_id_type=pl.DeviceIdType.MESH,
        )

    def across(offset, slot):
        return pltpu.make_async_remote_copy(
            src_ref=kv_all.at[slot], dst_ref=kv_all.at[slot],
            send_sem=i_send.at[offset], recv_sem=i_recv.at[offset],
            device_id={"wide": inner_peer}, device_id_type=pl.DeviceIdType.MESH,
        )

    @pl.loop(1, outer_n)
    def _(offset):
        along(offset, kv_all.at[wide], wide).start()

    across(0, wide).start()

    @pl.loop(1, outer_n)
    def _(offset):
        slot = outer_at(outer_n - offset)
        along(offset, kv_all.at[slot], slot).wait_recv()
        across(offset, slot).start()

    @pl.loop(0, outer_n)
    def _(offset):
        slot = outer_at(outer_n - offset)
        across(offset, slot + 1 - 2 * inner).wait_recv()
        across(offset, slot).wait_send()

    @pl.loop(1, outer_n)
    def _(offset):
        along(offset, kv_all.at[wide], wide).wait_send()

    for copy in sent:
        copy.wait_send()


def attention_kernel(length, queries, own_kv, cosine, sine, kv_all, kv_mine, out, kv_cache):
    question = pl.program_id(1)
    tokens = queries.shape[1]
    groups = queries.shape[2] // HD
    keys_n = kv_all.shape[0] * kv_all.shape[2]
    kv_cache[...] = kv_mine[...]
    cos, sin = cosine[0], sine[0]
    factor = HD ** (-0.5) * 1.4426950408889634
    cos_q, sin_q = cos * factor, sin * factor

    def rotate(rows, c, s):
        rows = rows.astype(F32)
        return (rows * c + pltpu.roll(rows, HD // 2, 1) * s).astype(BF16)

    own_key = rotate(own_kv[0, 0], cos, sin)
    own_value = own_kv[1, 0]
    pair = 2
    rows_n = tokens * pair
    causal = iota((rows_n, tokens), 0) % tokens >= iota((rows_n, tokens), 1)
    live = iota((rows_n, HD), 0) % tokens < length[question]
    for g in range(0, groups, pair):
        query = jnp.concatenate(
            [
                rotate(queries[0, :, HD * k : HD * (k + 1)], cos_q, sin_q)
                for k in range(g, g + pair)
            ],
            axis=0,
        )
        own = jnp.where(causal, dot_t(query, own_key), -1e30)
        scores = dot_t(query, kv_all[:, 0].reshape(keys_n, HD))
        top = jnp.maximum(
            jnp.max(scores, axis=1, keepdims=True), jnp.max(own, axis=1, keepdims=True)
        )
        weights = jnp.exp2(scores - top)
        own_w = jnp.exp2(own - top)
        denom = jnp.sum(weights, axis=1, keepdims=True) + jnp.sum(own_w, axis=1, keepdims=True)
        mixed = dot(weights.astype(BF16), kv_all[:, 1].reshape(keys_n, HD))
        mixed += dot(own_w.astype(BF16), own_value)
        mixed = jnp.where(live, mixed * (1.0 / denom), 0.0).astype(BF16)
        for k in range(pair):
            out[0, :, HD * (g + k) : HD * (g + k + 1)] = mixed[tokens * k : tokens * (k + 1)]


def both_halves(head_dim):
    freqs = np.power(1000000.0, -np.arange(head_dim // 2) * 2.0 / head_dim).astype(np.float32)
    return np.concatenate([freqs, freqs])


def turns(angles):
    half = angles.shape[-1] // 2
    sign = np.repeat(np.array([-1.0, 1.0], np.float32), half)
    return jnp.cos(angles), jnp.sin(angles) * sign


def mrope_angles(positions, head_dim):
    first_cut = head_dim // 8
    second_cut = first_cut + 3 * head_dim // 16
    place = positions.astype(F32)[:, :, None]
    lane = (np.arange(head_dim) % (head_dim // 2))[None, :]
    chosen = jnp.where(lane < first_cut, place[0], jnp.where(lane < second_cut, place[1], place[2]))
    return chosen * both_halves(head_dim)


def per_device(
    n_wide,
    patches,
    window_ids,
    vit_gain,
    vit_qkv,
    vit_qkv_bias,
    vit_proj,
    vit_proj_bias,
    merge_gain,
    merge_up,
    merge_up_bias,
    merge_down,
    merge_down_bias,
    input_gain,
    kv_weight,
    kv_bias,
    key_positions,
    queries,
    question_kv,
    question_start,
    question_length,
):
    rows_n, part_w = patches.shape
    patches = patches.T
    width = vit_proj.shape[1]
    block = rows_n // 4
    merged_block = block // 4
    d_wide = merge_down.shape[1]
    chunk = d_wide // CHUNKS
    hidden_n = merge_up.shape[1]
    kv_w = kv_weight.shape[2]
    key_cos, key_sin = turns(mrope_angles(key_positions, HD))
    tokens = queries.shape[1]
    place = (question_start[:, None] + jnp.arange(tokens, dtype=jnp.int32)[None, :]).astype(F32)
    query_cos, query_sin = turns(place[:, :, None] * both_halves(HD))

    vmem = pl.BlockSpec(memory_space=pltpu.VMEM)
    hbm = pl.BlockSpec(memory_space=pl.ANY)
    copies = 12 + 5 * CHUNKS
    kv_mine, kv_all = pl.pallas_call(
        functools.partial(vision_kernel, n_wide),
        out_shape=(
            jax.ShapeDtypeStruct((2, block, kv_w), BF16),
            jax.ShapeDtypeStruct((n_wide, 2, block, kv_w), BF16),
        ),
        in_specs=[vmem] * 12 + [hbm] * 5,
        out_specs=(vmem, vmem),
        scratch_shapes=[
            pltpu.VMEM((3, part_w, width), BF16),
            pltpu.VMEM(vit_proj.shape, BF16),
            pltpu.VMEM(merge_up.shape, BF16),
            pltpu.VMEM(merge_down.shape, BF16),
            pltpu.VMEM(kv_weight.shape, BF16),
            pltpu.SemaphoreType.DMA((5,)),
            pltpu.VMEM((4, part_w, rows_n), BF16),
            pltpu.VMEM((width, rows_n), BF16),
            pltpu.VMEM((part_w, rows_n), BF16),
            pltpu.VMEM((rows_n, width), F32),
            pltpu.VMEM((2, block, width), BF16),
            pltpu.VMEM((2, block, width), BF16),
            pltpu.VMEM((block, width), BF16),
            pltpu.VMEM((block, width), BF16),
            pltpu.VMEM((4, merged_block, 4 * width), BF16),
            pltpu.VMEM((block, hidden_n), F32),
            pltpu.VMEM((block, hidden_n), BF16),
            pltpu.VMEM((CHUNKS, block, chunk), F32),
            pltpu.VMEM((CHUNKS, 2, merged_block, chunk), BF16),
            pltpu.VMEM((CHUNKS, 2, merged_block, chunk), BF16),
            pltpu.VMEM((CHUNKS, merged_block, chunk), BF16),
            pltpu.VMEM((CHUNKS, merged_block, chunk), BF16),
            pltpu.VMEM((CHUNKS, 4, merged_block, chunk), BF16),
            pltpu.VMEM((4, merged_block, HD), F32),
            pltpu.VMEM((2, block, kv_w), F32),
            pltpu.SemaphoreType.DMA((copies,)),
            pltpu.SemaphoreType.DMA((copies,)),
            pltpu.SemaphoreType.DMA((n_wide // 2 - 1,)),
            pltpu.SemaphoreType.DMA((n_wide // 2 - 1,)),
            pltpu.SemaphoreType.DMA((n_wide // 2,)),
            pltpu.SemaphoreType.DMA((n_wide // 2,)),
        ],
        compiler_params=pltpu.CompilerParams(
            collective_id=0, has_side_effects=True, vmem_limit_bytes=VMEM_LIMIT
        ),
        name="vision_to_kv",
    )(
        window_ids,
        patches,
        vit_gain,
        vit_qkv_bias,
        vit_proj_bias,
        merge_gain,
        merge_up_bias,
        merge_down_bias.reshape(1, d_wide),
        input_gain.reshape(1, d_wide),
        kv_bias,
        key_cos,
        key_sin,
        vit_qkv.transpose(0, 2, 1),
        vit_proj,
        merge_up,
        merge_down,
        kv_weight,
    )
    q_count = queries.shape[0]
    kv_heads = kv_w // HD
    group_w = queries.shape[2] // kv_heads
    return pl.pallas_call(
        attention_kernel,
        grid_spec=pltpu.PrefetchScalarGridSpec(
            num_scalar_prefetch=1,
            grid=(kv_heads, q_count),
            in_specs=[
                pl.BlockSpec((1, tokens, group_w), lambda h, q, n: (q, 0, h)),
                pl.BlockSpec((2, 1, tokens, HD), lambda h, q, n: (0, q, 0, h)),
                pl.BlockSpec((1, tokens, HD), lambda h, q, n: (q, 0, 0)),
                pl.BlockSpec((1, tokens, HD), lambda h, q, n: (q, 0, 0)),
                pl.BlockSpec((n_wide, 2, block, HD), lambda h, q, n: (0, 0, 0, h)),
                pl.BlockSpec((2, block, HD), lambda h, q, n: (0, 0, h)),
            ],
            out_specs=(
                pl.BlockSpec((1, tokens, group_w), lambda h, q, n: (q, 0, h)),
                pl.BlockSpec((2, block, HD), lambda h, q, n: (0, 0, h)),
            ),
        ),
        out_shape=(
            jax.ShapeDtypeStruct(queries.shape, BF16),
            jax.ShapeDtypeStruct((2, block, kv_w), BF16),
        ),
        compiler_params=pltpu.CompilerParams(vmem_limit_bytes=VMEM_LIMIT),
        name="question_attention",
    )(question_length, queries, question_kv, query_cos, query_sin, kv_all, kv_mine)


def solution(mesh):
    return jax.shard_map(
        functools.partial(per_device, mesh.shape["wide"]),
        mesh=mesh,
        in_specs=(
            P("wide", "narrow"),
            P("wide", None),
            P(),
            P(None, None, "narrow"),
            P(None, "narrow"),
            P("narrow", None),
            P(),
            P(),
            P(None, "narrow"),
            P("narrow"),
            P("narrow", None),
            P(),
            P(),
            P(None, None, "narrow"),
            P(None, "narrow"),
            P(None, "wide"),
            P("wide", None, "narrow"),
            P(None, "wide", None, "narrow"),
            P("wide"),
            P("wide"),
        ),
        out_specs=(P("wide", None, "narrow"), P(None, "wide", "narrow")),
        check_vma=False,
    )
```

time: 102 us -> 87.4 us (0.86)
  the two profiles are of different devices: /device:TPU:13 before, /device:TPU:0 now
where the time goes in v2:
time: 87.4 us; the launch traced here: 87.2 us
  Pallas kernels  81.7 us (93%)
  other arithmetic  4.86 us (6%)
    pallas_call x1, Pallas kernels, per_device(): pl.pallas_call(functools.partial(vision_kernel, n_wide), out_shape=(jax.S...  66.6 us
    pallas_call x1, Pallas kernels, per_device(): pl.pallas_call(attention_kernel, grid_spec=pltpu.PrefetchScalarGridSpec(n...  15.1 us
    mul x2, other arithmetic, turns(): return (jnp.cos(angles), jnp.sin(angles) * sign)  3.45 us

profile of v2, /device:TPU:0, one launch (start us, length us, event | category | flops | bytes accessed | tf_op | source)
XLA Modules:
  0.0 87.2 jit_solution(5173052691855447050)
XLA Ops:
  0.6 0.7 convert_element_type.11
  1.3 0.7 add_convert_fusion
  2.0 1.6 %sine_multiply_fusion = (f32[64,128]{1,0:T(8,128)}, f32[64,128]{1,0:T(8,128)}) fusion(f32[128]{0:T(128)} %constant.11.clone, f32[128]{0:T(128)} %constant.10.clone, f32[64]{0:T(128)S(1)} %get-tuple-element.11, f32[64]{0:T(128)S(1)} %get-tuple-element.12, f32[64]{0:T(128)S(1)} %get-tuple-element.10, pred[128]{0:T(512)(128)(4,1)} %constant.18, ...), kind=kLoop, calls=%fused_computation.3 | loop fusion | flops 32768 | bytes 67584 | tf_op jit(solution)/shard_map/mul | solution.py:353
  3.6 1.9 %fusion = (f32[4,64,128]{2,1,0:T(8,128)}, f32[4,64,128]{2,1,0:T(8,128)}) fusion(f32[128]{0:T(128)} %constant.11.clone, f32[128]{0:T(128)} %constant.10.clone, f32[4,64]{1,0:T(4,128)S(1)} %add_convert_fusion), kind=kLoop, calls=%fused_computation.2 | loop fusion | flops 65536 | bytes 264192 | tf_op jit(solution)/shard_map/mul | solution.py:353
  5.5 66.6 %vision_to_kv.1 = (bf16[2,64,256]{2,1,0:T(8,128)(2,1)}, bf16[8,2,64,256]{3,2,1,0:T(8,128)(2,1)}) custom-call(s32[1,64]{1,0:T(1,128)} %ids.1, bf16[320,256]{1,0:T(8,128)(2,1)} %bitcast.11, f32[1280]{0:T(1024)} %gain.1, f32[3,320]{1,0:T(4,128)} %qkv_bias.1, f32[1280]{0:T(1024)} %proj_bias.1, f32[1280]{0:T(1024)} %merge_gain.1, f32[1280]{0:T(1024)} %up_bias.1, ...), custom_call_target="tpu_custom_call" | custom-call | tf_op jit(solution)/shard_map/vision_to_kv/pallas_call | solution.py:405
  72.1 15.1 %question_attention.1 = (bf16[4,64,2048]{2,1,0:T(8,128)(2,1)}, bf16[2,64,256]{2,1,0:T(8,128)(2,1)}) custom-call(s32[4]{0:T(128)} %length.1, bf16[4,64,2048]{2,1,0:T(8,128)(2,1)} %queries.1, bf16[2,4,64,256]{3,2,1,0:T(8,128)(2,1)} %own_kv.1, f32[4,64,128]{2,1,0:T(8,128)} %get-tuple-element.9.cosine, f32[4,64,128]{2,1,0:T(8,128)} %get-tuple-element.8.sine, ...), custom_call_target="tpu_custom_call" | custom-call | tf_op jit(solution)/shard_map/question_attention/pallas_call | solution.py:472
  (1 shorter events, 0.0 us)

commit v3 on v2

--- a/solution.py
+++ b/solution.py
@@ -1,4 +1,5 @@
 import functools
+import math
 
 import jax
 import jax.numpy as jnp
@@ -11,8 +12,11 @@
 HD = 128
 VHD = 80
 CHUNKS = 8
+PAIR = 4
+LAGS = (2, 5, 8, 10)
 F32 = jnp.float32
 BF16 = jnp.bfloat16
+PI_PARTS = (3.140625, 0.0009675025939941406, 1.5099580252808664e-07)
 VMEM_LIMIT = 60 * 1024 * 1024
 
 
@@ -43,15 +47,32 @@
     )
 
 
+def turns(angles):
+    turn = jnp.floor(angles * np.float32(1.0 / np.pi) + 0.5)
+    rest = ((angles - turn * PI_PARTS[0]) - turn * PI_PARTS[1]) - turn * PI_PARTS[2]
+    odd = turn - 2.0 * jnp.floor(turn * 0.5)
+    flip = 1.0 - 2.0 * odd
+    square = rest * rest
+    sine = rest
+    cosine = jnp.ones_like(rest)
+    s_sum, c_sum = jnp.zeros_like(rest), jnp.zeros_like(rest)
+    for k in range(7, 0, -1):
+        s_sum = (s_sum + (-1.0) ** k / math.factorial(2 * k + 1)) * square
+        c_sum = (c_sum + (-1.0) ** k / math.factorial(2 * k)) * square
+    sine = (sine + sine * s_sum) * flip
+    cosine = (cosine + c_sum) * flip
+    return cosine, jnp.where(iota(angles.shape, 1) < angles.shape[1] // 2, -sine, sine)
+
+
 def vision_kernel(
     n_wide,
     ids, patches, gain, qkv_bias, proj_bias, merge_gain, up_bias, down_bias, input_gain,
-    kv_bias, cosine, sine,
+    kv_bias, positions, freqs,
     qkv_hbm, proj_hbm, up_hbm, down_hbm, kvw_hbm,
     kv_out, kv_all,
     qkv_w, proj_w, up_w, down_w, kv_w, w_sem,
     rows, normed, heads, partial, give, got, x_give, x_got, merged, up_acc, up_act,
-    d_part, d_give, d_got, dx_give, dx_got, emb, squares, kv_acc,
+    d_part, d_give, d_got, dx_give, dx_got, emb, squares, kv_acc, key_cos, key_sin,
     send_sem, recv_sem, o_send, o_recv, i_send, i_recv,
 ):
     me = lax.axis_index("narrow")
@@ -137,6 +158,12 @@
         jnp.broadcast_to(ids_row, (8, row_count // 4)).astype(BF16), token_of.astype(BF16)
     )[:1]
     same = patch_col == patch_row
+    lane = iota((1, HD), 1) % (HD // 2)
+    places = [column(positions[k : k + 1, :].astype(F32)) for k in range(3)]
+    chosen = jnp.where(
+        lane < HD // 8, places[0], jnp.where(lane < HD // 8 + 3 * HD // 16, places[1], places[2])
+    )
+    key_cos[...], key_sin[...] = turns(chosen * freqs[...])
     gather_forward(0, rows)
     gather_finish(0, rows)
     loads[3].start()
@@ -210,21 +237,21 @@
     loads[3].wait()
     kv_acc[...] = jnp.zeros_like(kv_acc)
     square_sum = jnp.zeros((merged_block, 1), F32)
-    for t in range(CHUNKS + 4):
+    for t in range(CHUNKS + LAGS[3]):
         c = t
         if c < CHUNKS:
             d_part[c] = dot(up_act[...], down_w[:, chunk * c : chunk * (c + 1)])
             d_give[c, 0] = rows_of(d_part.at[c], dg, merged_block).astype(BF16)
             d_give[c, 1] = rows_of(d_part.at[c], cp, merged_block).astype(BF16)
             send(12 + 5 * c, d_give.at[c], d_got.at[c], cp)
-        c = t - 1
+        c = t - LAGS[0]
         if 0 <= c < CHUNKS:
             arrived(12 + 5 * c, d_got.at[c], cp)
             dx_give[c] = (
                 rows_of(d_part.at[c], xp, merged_block) + d_got[c, 0].astype(F32)
             ).astype(BF16)
             send(13 + 5 * c, dx_give.at[c], dx_got.at[c], xp)
-        c = t - 2
+        c = t - LAGS[1]
         if 0 <= c < CHUNKS:
             arrived(13 + 5 * c, dx_got.at[c], xp)
             cols = slice(chunk * c, chunk * (c + 1))
@@ -236,12 +263,12 @@
             if c == CHUNKS - 1:
                 squares[me] = jnp.broadcast_to(square_sum, squares.shape[1:])
                 gather_start(9, squares.at[me], squares)
-        c = t - 3
+        c = t - LAGS[2]
         if 0 <= c < CHUNKS:
             gather_forward(14 + 5 * c, emb.at[c])
             if c == CHUNKS - 1:
                 gather_forward(9, squares)
-        c = t - 4
+        c = t - LAGS[3]
         if 0 <= c < CHUNKS:
             gather_finish(14 + 5 * c, emb.at[c])
             if c == 0:
@@ -254,7 +281,7 @@
     for h in range(kv_w.shape[2] // HD):
         cols = slice(HD * h, HD * (h + 1))
         raw = kv_acc[0, :, cols] * row_scale + kv_bias[0:1, cols]
-        rotated = raw * cosine[...] + pltpu.roll(raw, HD // 2, 1) * sine[...]
+        rotated = raw * key_cos[...] + pltpu.roll(raw, HD // 2, 1) * key_sin[...]
         kv_out[0, :, cols] = rotated.astype(BF16)
         kv_out[1, :, cols] = (kv_acc[1, :, cols] * row_scale + kv_bias[1:2, cols]).astype(BF16)
     kv_all[wide] = kv_out[...]
@@ -299,67 +326,58 @@
         copy.wait_send()
 
 
-def attention_kernel(length, queries, own_kv, cosine, sine, kv_all, kv_mine, out, kv_cache):
+def attention_kernel(
+    length, start, queries, own_kv, freqs, kv_all, kv_mine, out, kv_cache, keys_t, values
+):
     question = pl.program_id(1)
     tokens = queries.shape[1]
     groups = queries.shape[2] // HD
     keys_n = kv_all.shape[0] * kv_all.shape[2]
-    kv_cache[...] = kv_mine[...]
-    cos, sin = cosine[0], sine[0]
+
+    @pl.when(question == 0)
+    def _():
+        kv_cache[...] = kv_mine[...]
+        keys_t[...] = kv_all[:, 0].reshape(keys_n, HD).astype(F32).T.astype(BF16)
+        values[:, :HD] = kv_all[:, 1].reshape(keys_n, HD)
+        values[:, HD:] = jnp.ones((keys_n, HD), BF16)
+
+    place = (start[question] + iota((tokens, HD), 0)).astype(F32)
+    cos, sin = turns(place * freqs[...])
     factor = HD ** (-0.5) * 1.4426950408889634
     cos_q, sin_q = cos * factor, sin * factor
 
     def rotate(rows, c, s):
         rows = rows.astype(F32)
-        return (rows * c + pltpu.roll(rows, HD // 2, 1) * s).astype(BF16)
-
-    own_key = rotate(own_kv[0, 0], cos, sin)
-    own_value = own_kv[1, 0]
-    pair = 2
-    rows_n = tokens * pair
+        return rows * c + pltpu.roll(rows, HD // 2, 1) * s
+
+    own_key = rotate(own_kv[0, 0], cos, sin).T.astype(BF16)
+    own_value = jnp.concatenate([own_kv[1, 0], jnp.ones((tokens, HD), BF16)], axis=1)
+    rows_n = tokens * PAIR
     causal = iota((rows_n, tokens), 0) % tokens >= iota((rows_n, tokens), 1)
     live = iota((rows_n, HD), 0) % tokens < length[question]
-    for g in range(0, groups, pair):
+    for g in range(0, groups, PAIR):
         query = jnp.concatenate(
             [
-                rotate(queries[0, :, HD * k : HD * (k + 1)], cos_q, sin_q)
-                for k in range(g, g + pair)
+                rotate(queries[0, :, HD * k : HD * (k + 1)], cos_q, sin_q).astype(BF16)
+                for k in range(g, g + PAIR)
             ],
             axis=0,
         )
-        own = jnp.where(causal, dot_t(query, own_key), -1e30)
-        scores = dot_t(query, kv_all[:, 0].reshape(keys_n, HD))
+        own = jnp.where(causal, dot(query, own_key), -1e30)
+        scores = dot(query, keys_t[...])
         top = jnp.maximum(
             jnp.max(scores, axis=1, keepdims=True), jnp.max(own, axis=1, keepdims=True)
         )
-        weights = jnp.exp2(scores - top)
-        own_w = jnp.exp2(own - top)
-        denom = jnp.sum(weights, axis=1, keepdims=True) + jnp.sum(own_w, axis=1, keepdims=True)
-        mixed = dot(weights.astype(BF16), kv_all[:, 1].reshape(keys_n, HD))
-        mixed += dot(own_w.astype(BF16), own_value)
-        mixed = jnp.where(live, mixed * (1.0 / denom), 0.0).astype(BF16)
-        for k in range(pair):
+        mixed = dot(jnp.exp2(scores - top).astype(BF16), values[...])
+        mixed += dot(jnp.exp2(own - top).astype(BF16), own_value)
+        mixed = jnp.where(live, mixed[:, :HD] / mixed[:, HD:], 0.0).astype(BF16)
+        for k in range(PAIR):
             out[0, :, HD * (g + k) : HD * (g + k + 1)] = mixed[tokens * k : tokens * (k + 1)]
 
 
 def both_halves(head_dim):
     freqs = np.power(1000000.0, -np.arange(head_dim // 2) * 2.0 / head_dim).astype(np.float32)
     return np.concatenate([freqs, freqs])
-
-
-def turns(angles):
-    half = angles.shape[-1] // 2
-    sign = np.repeat(np.array([-1.0, 1.0], np.float32), half)
-    return jnp.cos(angles), jnp.sin(angles) * sign
-
-
-def mrope_angles(positions, head_dim):
-    first_cut = head_dim // 8
-    second_cut = first_cut + 3 * head_dim // 16
-    place = positions.astype(F32)[:, :, None]
-    lane = (np.arange(head_dim) % (head_dim // 2))[None, :]
-    chosen = jnp.where(lane < first_cut, place[0], jnp.where(lane < second_cut, place[1], place[2]))
-    return chosen * both_halves(head_dim)
 
 
 def per_device(
@@ -394,10 +412,8 @@
     chunk = d_wide // CHUNKS
     hidden_n = merge_up.shape[1]
     kv_w = kv_weight.shape[2]
-    key_cos, key_sin = turns(mrope_angles(key_positions, HD))
     tokens = queries.shape[1]
-    place = (question_start[:, None] + jnp.arange(tokens, dtype=jnp.int32)[None, :]).astype(F32)
-    query_cos, query_sin = turns(place[:, :, None] * both_halves(HD))
+    freqs = jnp.asarray(both_halves(HD)[None, :])
 
     vmem = pl.BlockSpec(memory_space=pltpu.VMEM)
     hbm = pl.BlockSpec(memory_space=pl.ANY)
@@ -436,6 +452,8 @@
             pltpu.VMEM((CHUNKS, 4, merged_block, chunk), BF16),
             pltpu.VMEM((4, merged_block, HD), F32),
             pltpu.VMEM((2, block, kv_w), F32),
+            pltpu.VMEM((block, HD), F32),
+            pltpu.VMEM((block, HD), F32),
             pltpu.SemaphoreType.DMA((copies,)),
             pltpu.SemaphoreType.DMA((copies,)),
             pltpu.SemaphoreType.DMA((n_wide // 2 - 1,)),
@@ -458,8 +476,8 @@
         merge_down_bias.reshape(1, d_wide),
         input_gain.reshape(1, d_wide),
         kv_bias,
-        key_cos,
-        key_sin,
+        key_positions,
+        freqs,
         vit_qkv.transpose(0, 2, 1),
         vit_proj,
         merge_up,
@@ -472,20 +490,23 @@
     return pl.pallas_call(
         attention_kernel,
         grid_spec=pltpu.PrefetchScalarGridSpec(
-            num_scalar_prefetch=1,
+            num_scalar_prefetch=2,
             grid=(kv_heads, q_count),
             in_specs=[
-                pl.BlockSpec((1, tokens, group_w), lambda h, q, n: (q, 0, h)),
-                pl.BlockSpec((2, 1, tokens, HD), lambda h, q, n: (0, q, 0, h)),
-                pl.BlockSpec((1, tokens, HD), lambda h, q, n: (q, 0, 0)),
-                pl.BlockSpec((1, tokens, HD), lambda h, q, n: (q, 0, 0)),
-                pl.BlockSpec((n_wide, 2, block, HD), lambda h, q, n: (0, 0, 0, h)),
-                pl.BlockSpec((2, block, HD), lambda h, q, n: (0, 0, h)),
+                pl.BlockSpec((1, tokens, group_w), lambda h, q, n, p: (q, 0, h)),
+                pl.BlockSpec((2, 1, tokens, HD), lambda h, q, n, p: (0, q, 0, h)),
+                pl.BlockSpec((1, HD), lambda h, q, n, p: (0, 0)),
+                pl.BlockSpec((n_wide, 2, block, HD), lambda h, q, n, p: (0, 0, 0, h)),
+                pl.BlockSpec((2, block, HD), lambda h, q, n, p: (0, 0, h)),
             ],
             out_specs=(
-                pl.BlockSpec((1, tokens, group_w), lambda h, q, n: (q, 0, h)),
-                pl.BlockSpec((2, block, HD), lambda h, q, n: (0, 0, h)),
+                pl.BlockSpec((1, tokens, group_w), lambda h, q, n, p: (q, 0, h)),
+                pl.BlockSpec((2, block, HD), lambda h, q, n, p: (0, 0, h)),
             ),
+            scratch_shapes=[
+                pltpu.VMEM((HD, n_wide * block), BF16),
+                pltpu.VMEM((n_wide * block, 2 * HD), BF16),
+            ],
         ),
         out_shape=(
             jax.ShapeDtypeStruct(queries.shape, BF16),
@@ -493,7 +514,7 @@
         ),
         compiler_params=pltpu.CompilerParams(vmem_limit_bytes=VMEM_LIMIT),
         name="question_attention",
-    )(question_length, queries, question_kv, query_cos, query_sin, kv_all, kv_mine)
+    )(question_length, question_start, queries, question_kv, freqs, kv_all, kv_mine)
 
 
 def solution(mesh):

time: 87.4 us -> 71.6 us (0.82)
  Pallas kernels: 81.7 us -> 70.8 us
  other arithmetic: 4.86 us -> 0 us
    pallas_call x1, Pallas kernels: 66.6 us -> 60.2 us  [per_device(): pl.pallas_call(functools.partial(vision_kernel, n_wide), out_shape=(jax.S...]
    pallas_call x1, Pallas kernels: 15.1 us -> 10.6 us  [per_device(): pl.pallas_call(attention_kernel, grid_spec=pltpu.PrefetchScalarGridSpec(n...]
    mul x2 -> x0, other arithmetic: 3.45 us -> none  [turns(): return (jnp.cos(angles), jnp.sin(angles) * sign)]
    convert_element_type x2 -> x0, other arithmetic: 1.41 us -> none  [the longest x1 0.73 us: per_device(): (question_start[:, None] + jnp.arange(tokens, dtype=jnp.int32)[None, :])....]
where the time goes in v3:
time: 71.6 us; the launch traced here: 71.4 us
  Pallas kernels  70.8 us (99%)
    pallas_call x1, Pallas kernels, per_device(): pl.pallas_call(functools.partial(vision_kernel, n_wide), out_shape=(jax.S...  60.2 us
    pallas_call x1, Pallas kernels, per_device(): pl.pallas_call(attention_kernel, grid_spec=pltpu.PrefetchScalarGridSpec(n...  10.6 us

profile of v3, /device:TPU:0, one launch (start us, length us, event | category | flops | bytes accessed | tf_op | source)
XLA Modules:
  0.0 71.4 jit_solution(3917625889763833285)
XLA Ops:
  0.6 60.2 %vision_to_kv.1 = (bf16[2,64,256]{2,1,0:T(8,128)(2,1)}, bf16[8,2,64,256]{3,2,1,0:T(8,128)(2,1)}) custom-call(s32[1,64]{1,0:T(1,128)} %ids.1, bf16[320,256]{1,0:T(8,128)(2,1)} %bitcast.5, f32[1280]{0:T(1024)} %gain.1, f32[3,320]{1,0:T(4,128)} %qkv_bias.1, f32[1280]{0:T(1024)} %proj_bias.1, f32[1280]{0:T(1024)} %merge_gain.1, f32[1280]{0:T(1024)} %up_bias.1, ...), custom_call_target="tpu_custom_call" | custom-call | tf_op jit(solution)/shard_map/vision_to_kv/pallas_call | solution.py:421
  60.8 10.6 %question_attention.1 = (bf16[4,64,2048]{2,1,0:T(8,128)(2,1)}, bf16[2,64,256]{2,1,0:T(8,128)(2,1)}) custom-call(s32[4]{0:T(128)} %length.1, s32[4]{0:T(128)} %start.1, bf16[4,64,2048]{2,1,0:T(8,128)(2,1)} %queries.1, bf16[2,4,64,256]{3,2,1,0:T(8,128)(2,1)} %own_kv.1, f32[1,128]{1,0:T(1,128)} %constant.2.clone.freqs, ...), custom_call_target="tpu_custom_call" | custom-call | tf_op jit(solution)/shard_map/question_attention/pallas_call | solution.py:490
